TPU v7x, 32 devices: a whole 2x2x4 slice. The times are simulated.
32 devices in a mesh: grp: 2 (over y), surf: 4 (over z), ang: 2 (over x), row: 2 (over core).
Axes of the slice: x: 2, y: 2, z: 4, core: 2. Of those that a mesh axis runs over, the one named last changes fastest.
Arguments:
- incident: bfloat16 [256, 32768], P(('grp', 'ang'), 'surf'), parts along dimension 0, may hold values from -6 to 6
- near_blocks: bfloat16 [512, 4, 128, 128], P(('grp', 'surf', 'row')), parts along dimension 0, may hold values from -0.25 to 0.25
- near_cols: int32 [512, 4], P(('grp', 'surf', 'row')), parts along dimension 0, may hold values from 0 to 95
- gram_inv: bfloat16 [512, 128, 128], P(('grp', 'surf', 'row')), parts along dimension 0, may hold values from -0.5 to 0.5
- prolong: bfloat16 [512, 128, 768], P(('grp', 'surf')), parts along dimension 0, may hold values from -0.5 to 0.5
- dual_blocks: bfloat16 [3072, 3, 128, 128], P(('grp', 'surf', 'row')), parts along dimension 0, may hold values from -0.3125 to 0.3125
- dual_cols: int32 [3072, 3], P(('grp', 'surf', 'row')), parts along dimension 0, may hold values from 0 to 575
- dual_count: int32 [3072], P(('grp', 'surf', 'row')), parts along dimension 0, may hold values from 1 to 3, as said below
- primal_border: int32 [8, 2, 16], P(('grp', 'surf')), parts along dimension 0, may hold values from 0 to 63, as said below
- fine_border: int32 [8, 2, 96], P(('grp', 'surf')), parts along dimension 0, may hold values from 0 to 383, as said below
Outputs:
- preconditioned: float32 [256, 32768], P(('grp', 'ang'), ('surf', 'row')), parts along dimension 0
There are 2 independent parts, one for each index of `grp`. A program takes and returns all parts, laid end to end along the dimension named above; each array names one. Nothing has to cross between parts.
Inputs may be any that keep to these rules, and one draw needn't show every extreme that they name: near_cols indexes the 64 own blocks, then the 16 received from the partition before, then the 16 from the one after. dual_cols indexes the 384 own fine blocks, then the 96 received from the partition before, then the 96 from the one after. Only the first dual_count[f] blocks and column indices of row f count; every half of a partition's fine rows has a row with 3. `primal_border`: the 32 blocks listed for one partition are distinct. `fine_border`: the 192 fine blocks listed for one partition are distinct.
All inputs are finite; a program needn't handle non-finite values.
Results may differ from a plain program's by a relative error of at most 0.0064.
Values may be sent and summed in bfloat16 or wider, within the bound.
A program may use at most 192 MiB of HBM per device.

v0:
```python
import jax
import jax.numpy as jnp
from jax import lax
from jax.sharding import PartitionSpec as P


def padded_2(cells, sides, width):
    for axis, dim in sides:
        count = lax.axis_size(axis)
        head = lax.slice_in_dim(cells, 0, width, axis=dim)
        tail = lax.slice_in_dim(cells, cells.shape[dim] - width, cells.shape[dim], axis=dim)
        cells = jnp.concatenate(
            [
                lax.ppermute(tail, axis, [(i, (i + 1) % count) for i in range(count)]),
                cells,
                lax.ppermute(head, axis, [((i + 1) % count, i) for i in range(count)]),
            ],
            axis=dim,
        )
    return cells


def dual_product(source_field, matrices, indices, counts, block_size):
    blocks = source_field.reshape(source_field.shape[0], -1, block_size)
    picked = jnp.take(blocks, indices, axis=1)
    live_mask = jnp.arange(indices.shape[1])[None, :] < counts[:, None]
    picked = jnp.where(live_mask[None, :, :, None], picked, jnp.zeros((), picked.dtype))
    return jnp.einsum(
        "cfkb,fkbe->cfe", picked, matrices, preferred_element_type=jnp.float32
    ).astype(jnp.bfloat16)


def body(
    incident,
    near_blocks,
    near_cols,
    gram_inv,
    prolong,
    dual_blocks,
    dual_cols,
    dual_count,
    primal_border,
    fine_border,
):
    columns = incident.shape[0]
    block_size = prolong.shape[1]
    coarse = prolong.shape[0]
    fine_per = prolong.shape[2] // block_size
    half_rows = near_blocks.shape[0]
    rim_blocks = primal_border.shape[2]
    fine_rim = fine_border.shape[2]
    blocks = incident.reshape(columns, coarse, block_size)
    outgoing = jnp.take(blocks, primal_border[0].reshape(-1), axis=1).reshape(
        columns, 2 * rim_blocks * block_size
    )
    padded = padded_2(outgoing, (("surf", 1),), rim_blocks * block_size)
    extended = jnp.concatenate(
        [incident, padded[:, : rim_blocks * block_size], padded[:, 3 * rim_blocks * block_size :]],
        axis=1,
    )
    extended = extended.reshape(columns, coarse + 2 * rim_blocks, block_size)
    picked = jnp.take(extended, near_cols, axis=1)
    applied = jnp.einsum(
        "cikb,ikbe->cie", picked, near_blocks, preferred_element_type=jnp.float32
    ).astype(jnp.bfloat16)
    mapped = jnp.einsum(
        "cib,ibe->cie", applied, gram_inv, preferred_element_type=jnp.float32
    ).astype(jnp.bfloat16)
    first_block = lax.axis_index("row") * half_rows
    own_prolong = lax.dynamic_slice_in_dim(prolong, first_block, half_rows, 0)
    part_fine = jnp.einsum(
        "cib,ibe->cie", mapped, own_prolong, preferred_element_type=jnp.float32
    ).astype(jnp.bfloat16)
    part_fine = part_fine.reshape(columns, half_rows * fine_per * block_size)
    refined = lax.all_gather(part_fine, "row", axis=1, tiled=True)
    fine_blocks = refined.reshape(columns, coarse * fine_per, block_size)
    sending = jnp.take(fine_blocks, fine_border[0].reshape(-1), axis=1).reshape(
        columns, 2 * fine_rim * block_size
    )
    edge_cells = padded_2(sending, (("surf", 1),), fine_rim * block_size)
    dual_field = jnp.concatenate(
        [
            refined,
            edge_cells[:, : fine_rim * block_size],
            edge_cells[:, 3 * fine_rim * block_size :],
        ],
        axis=1,
    )
    response = dual_product(dual_field, dual_blocks, dual_cols, dual_count, block_size)
    response = response.reshape(columns, half_rows, fine_per * block_size)
    collapsed = jnp.einsum(
        "cie,ibe->cib", response, own_prolong, preferred_element_type=jnp.float32
    ).astype(jnp.bfloat16)
    result = jnp.einsum("cib,ieb->cie", collapsed, gram_inv, preferred_element_type=jnp.float32)
    return result.reshape(columns, half_rows * block_size)


def solution(mesh):
    return jax.shard_map(
        body,
        mesh=mesh,
        in_specs=(
            P(("grp", "ang"), "surf"),
            P(("grp", "surf", "row"), None, None, None),
            P(("grp", "surf", "row"), None),
            P(("grp", "surf", "row"), None, None),
            P(("grp", "surf"), None, None),
            P(("grp", "surf", "row"), None, None, None),
            P(("grp", "surf", "row"), None),
            P(("grp", "surf", "row")),
            P(("grp", "surf"), None, None),
            P(("grp", "surf"), None, None),
        ),
        out_specs=P(("grp", "ang"), ("surf", "row")),
        check_vma=False,
    )
```

profile of v0, /device:TPU:0, one launch (start us, length us, event | category | flops | bytes accessed | tf_op | source)
XLA Modules:
  0.0 213.5 jit_solution(6894475617880481124)
XLA Ops:
  6.5 0.0 copy-start
  6.5 0.0 all-gather.2.cloned.1.call-start
  6.5 0.9 reshape_squeeze.11
  7.4 0.8 reshape_squeeze.10
  8.2 1.5 copy_bitcast_fusion.4
  9.7 0.1 broadcast_bitcast_fusion.1
  9.8 0.6 gather_fusion
  10.4 0.1 bitcast_select_fusion.1
  10.6 3.1 %collective-permute-start = (bf16[64,2048]{1,0:T(8,128)(2,1)S(1)}, bf16[64,2048]{1,0:T(8,128)(2,1)S(1)}, u32[]{:S(2)}, u32[]{:S(2)}) collective-permute-start(bf16[64,2048]{1,0:T(8,128)(2,1)S(1)} %get-tuple-element.7), channel_id=1, source_target_pairs={{0,4},{4,8},{8,12},{12,0},{1,5},{5,9},{9,13},{13,1},{2,6},{6,10},{... | collective-permute-start | bytes 786440 | tf_op jit(solution)/shard_map/ppermute | solution.py:14
  13.7 2.1 collective-permute-start.1
  15.8 0.0 copy-done.2
  15.8 0.1 copy.25
  15.9 0.1 reshape.143
  16.0 0.1 copy.22
  16.1 6.8 %collective-permute-done = bf16[64,2048]{1,0:T(8,128)(2,1)S(1)} collective-permute-done((bf16[64,2048]{1,0:T(8,128)(2,1)S(1)}, bf16[64,2048]{1,0:T(8,128)(2,1)S(1)}, u32[]{:S(2)}, u32[]{:S(2)}) %collective-permute-start) | collective-permute-done | bytes 262176 | tf_op jit(solution)/shard_map/ppermute | solution.py:14
  22.9 4.2 %collective-permute-done.1 = bf16[64,2048]{1,0:T(8,128)(2,1)S(1)} collective-permute-done((bf16[64,2048]{1,0:T(8,128)(2,1)S(1)}, bf16[64,2048]{1,0:T(8,128)(2,1)S(1)}, u32[]{:S(2)}, u32[]{:S(2)}) %collective-permute-start.1) | collective-permute-done | bytes 262176 | tf_op jit(solution)/shard_map/ppermute | solution.py:16
  27.1 1.7 copy_bitcast_fusion.2
  28.7 2.1 %gather_fusion.1 = bf16[128,64,128]{2,1,0:T(8,128)(2,1)} fusion(bf16[64,96,128]{2,0,1:T(8,128)(2,1)S(1)} %copy_bitcast_fusion.2, s32[1024]{0:T(1024)S(1)} %pad_clamp_fusion.2), kind=kCustom, calls=%fused_computation.1 | custom fusion | bytes 4194816 | tf_op jit(solution)/shard_map/jit(_take)/gather | solution.py:62
  30.9 4.0 %fusion.38 = bf16[64,32,128]{2,0,1:T(8,128)(2,1)S(1)} fusion(bf16[32,128,128]{2,1,0:T(8,128)(2,1)S(1)} %copy-done, bf16[32,4,128,128]{3,2,1,0:T(8,128)(2,1)} %param.11, bf16[32,4,64,128]{3,2,1,0:T(8,128)(2,1)} %bitcast.100, pred[32,4]{1,0:T(8,128)(4,1)S(1)} %copy.22), kind=kOutput, calls=%fused_computation.36 | convolution fusion | flops 337117184 | bytes 7864448 | tf_op jit(solution)/shard_map/cib,ibe->cie/dot_general | solution.py:66
  34.9 3.8 %convert_bitcast_fusion = bf16[32,8,8,768]{3,2,1,0:T(8,128)(2,1)S(1)} fusion(bf16[64,32,128]{2,0,1:T(8,128)(2,1)S(1)} %fusion.38, bf16[64,128,768]{2,1,0:T(8,128)(2,1)} %param.14, s32[]{:T(128)S(6)} %select_n.67), kind=kOutput, calls=%fused_computation.23 | convolution fusion | flops 404226048 | bytes 9961476 | tf_op jit(solution)/shard_map/cib,ibe->cie/dot_general | solution.py:71
  38.7 1.8 copy.42
  40.6 0.0 all-gather.2.cloned.1.call-update
  40.6 0.7 copy-done.3
  41.2 0.1 reshape_squeeze.13
  41.3 0.1 reshape_squeeze.12
  41.4 0.1 broadcast_bitcast_fusion
  41.5 15.9 %all-gather.2.cloned.1.call-done = bf16[64,49152]{1,0:T(8,128)(2,1)} async-done(((bf16[64,24576]{1,0:T(8,128)(2,1)}), bf16[64,49152]{1,0:T(8,128)(2,1)}) %all-gather.2.cloned.1.call-update) | async-done | bytes 6291472 | tf_op jit(solution)/shard_map/all_gather | solution.py:75
  57.5 7.2 %copy_bitcast_fusion.1 = bf16[64,384,128]{2,0,1:T(8,128)(2,1)} fusion(bf16[64,49152]{1,0:T(8,128)(2,1)} %all-gather.2.cloned.1.call-done), kind=kLoop, calls=%fused_computation.12 | loop fusion | bytes 12582912 | tf_op jit(solution)/shard_map/reshape | solution.py:76
  64.7 5.6 %gather_fusion.2 = bf16[192,64,128]{2,1,0:T(8,128)(2,1)} fusion(bf16[64,384,128]{2,0,1:T(8,128)(2,1)} %copy_bitcast_fusion.1, s32[1024]{0:T(1024)S(1)} %pad_clamp_fusion.1), kind=kCustom, calls=%fused_computation.2 | custom fusion | bytes 6292224 | tf_op jit(solution)/shard_map/jit(_take)/gather | solution.py:77
  70.3 2.5 %bitcast_select_fusion = bf16[64,24576]{1,0:T(8,128)(2,1)S(1)} fusion(pred[24576]{0:T(1024)(128)(4,1)S(1)} %broadcast_bitcast_fusion, bf16[192,64,128]{2,1,0:T(8,128)(2,1)} %gather_fusion.2), kind=kLoop, calls=%fused_computation.21 | loop fusion | flops 1572864 | bytes 6316032 | tf_op jit(solution)/shard_map/jit(_take)/select_n | solution.py:77
  72.7 0.0 copy-start.1
  72.7 0.0 copy-start.4
  72.8 1.8 fusion.58
  74.6 1.7 collective-permute-start.2
  76.3 2.1 collective-permute-start.3
  78.4 0.1 copy.30
  78.6 0.2 reshape.159
  78.8 0.2 copy.21
  79.0 0.1 iota_compare_fusion
  79.1 34.8 %collective-permute-done.2 = bf16[64,12288]{1,0:T(8,128)(2,1)S(1)} collective-permute-done((bf16[64,12288]{1,0:T(8,128)(2,1)}, bf16[64,12288]{1,0:T(8,128)(2,1)S(1)}, u32[]{:S(2)}, u32[]{:S(2)}) %collective-permute-start.2) | collective-permute-done | bytes 1572896 | tf_op jit(solution)/shard_map/ppermute | solution.py:14
  113.9 32.8 %collective-permute-done.3 = bf16[64,12288]{1,0:T(8,128)(2,1)} collective-permute-done((bf16[64,12288]{1,0:T(8,128)(2,1)}, bf16[64,12288]{1,0:T(8,128)(2,1)}, u32[]{:S(2)}, u32[]{:S(2)}) %collective-permute-start.3) | collective-permute-done | bytes 1572896 | tf_op jit(solution)/shard_map/ppermute | solution.py:16
  146.7 7.8 %copy_bitcast_fusion = bf16[64,576,128]{2,0,1:T(8,128)(2,1)} fusion(bf16[64,12288]{1,0:T(8,128)(2,1)} %collective-permute-done.3, bf16[64,12288]{1,0:T(8,128)(2,1)S(1)} %collective-permute-done.2, bf16[64,49152]{1,0:T(8,128)(2,1)} %all-gather.2.cloned.1.call-done), kind=kLoop, calls=%fused_computation.4 | loop fusion | flops 28311552 | bytes 18874368 | tf_op jit(solution)/shard_map/reshape | solution.py:24
  154.4 23.3 %gather_fusion.3 = bf16[576,64,128]{2,1,0:T(8,128)(2,1)} fusion(bf16[64,576,128]{2,0,1:T(8,128)(2,1)} %copy_bitcast_fusion, s32[1024]{0:T(1024)S(1)} %pad_clamp_fusion), kind=kCustom, calls=%fused_computation.3 | custom fusion | bytes 18876672 | tf_op jit(solution)/shard_map/jit(_take)/gather | solution.py:25
  177.8 11.1 %fusion.12 = bf16[64,192,128]{2,0,1:T(8,128)(2,1)S(1)} fusion(bf16[192,3,128,128]{3,2,1,0:T(8,128)(2,1)} %param.15, bf16[192,3,64,128]{3,2,1,0:T(8,128)(2,1)} %bitcast.98, pred[192,3]{1,0:T(8,128)(4,1)S(1)} %iota_compare_fusion, pred[192,3]{1,0:T(8,128)(4,1)S(1)} %copy.21), kind=kOutput, calls=%fused_computation.20 | convolution fusion | flops 1218969600 | bytes 31458432 | tf_op jit(solution)/shard_map/cfkb,fkbe->cfe/dot_general | solution.py:28
  188.8 3.7 %copy.32 = bf16[64,192,128]{2,1,0:T(8,128)(2,1)} copy(bf16[64,192,128]{2,0,1:T(8,128)(2,1)S(1)} %fusion.12) | data formatting | bytes 6291456 | tf_op jit(solution)/shard_map/convert_element_type | solution.py:30
  192.5 6.4 %reshape.131 = bf16[64,32,768]{2,1,0:T(8,128)(2,1)} reshape(bf16[64,192,128]{2,1,0:T(8,128)(2,1)} %copy.32) | data formatting | bytes 6291456 | tf_op jit(solution)/shard_map/reshape | solution.py:90
  198.9 6.7 %convolution_bitcast_fusion = f32[32,8,8,128]{3,2,1,0:T(8,128)S(1)} fusion(bf16[32,128,128]{2,1,0:T(8,128)(2,1)S(1)} %copy-done, bf16[64,32,768]{2,1,0:T(8,128)(2,1)} %reshape.131, bf16[64,128,768]{2,1,0:T(8,128)(2,1)} %param.14, s32[]{:T(128)S(6)} %select_n.67), kind=kOutput, calls=%fused_computation.31 | convolution fusion | flops 470024192 | bytes 11534340 | tf_op jit(solution)/shard_map/cib,ieb->cie/dot_general | solution.py:94
  205.6 1.0 copy.60
  (18 shorter events, 0.1 us)
Async XLA Ops:
  6.5 24.3 %copy-start = (bf16[32,128,128]{2,1,0:T(8,128)(2,1)S(1)}, bf16[32,128,128]{2,1,0:T(8,128)(2,1)}, u32[]{:S(2)}) copy-start(bf16[32,128,128]{2,1,0:T(8,128)(2,1)} %param.13) | copy-start | bytes 3145732
  6.5 9.2 %copy-start.2 = (s32[32,4]{0,1:T(4,128)S(1)}, s32[32,4]{0,1:T(4,128)}, u32[]{:S(2)}) copy-start(s32[32,4]{0,1:T(4,128)} %param.12) | copy-start | bytes 1540
  6.5 50.9 %all-gather.2.cloned.1.call-start = ((), (), s32[]{:S(2)}) async-start(), calls=%async_computation | async-start | bytes 9437184 | tf_op jit(solution)/shard_map/all_gather | solution.py:75
  10.6 12.3 %collective-permute-start = (bf16[64,2048]{1,0:T(8,128)(2,1)S(1)}, bf16[64,2048]{1,0:T(8,128)(2,1)S(1)}, u32[]{:S(2)}, u32[]{:S(2)}) collective-permute-start(bf16[64,2048]{1,0:T(8,128)(2,1)S(1)} %get-tuple-element.7), channel_id=1, source_target_pairs={{0,4},{4,8},{8,12},{12,0},{1,5},{5,9},{9,13},{13,1},{2,6},{6,10},{... | collective-permute-start | bytes 786440 | tf_op jit(solution)/shard_map/ppermute | solution.py:14
  13.7 13.4 %collective-permute-start.1 = (bf16[64,2048]{1,0:T(8,128)(2,1)S(1)}, bf16[64,2048]{1,0:T(8,128)(2,1)S(1)}, u32[]{:S(2)}, u32[]{:S(2)}) collective-permute-start(bf16[64,2048]{1,0:T(8,128)(2,1)S(1)} %get-tuple-element.8), channel_id=1, source_target_pairs={{4,0},{8,4},{12,8},{0,12},{5,1},{9,5},{13,9},{1,13},{6,2},{10,6},{... | collective-permute-start | bytes 786440 | tf_op jit(solution)/shard_map/ppermute | solution.py:16
  40.6 0.7 copy-start.3
  72.7 5.7 %copy-start.1 = (s32[192,3]{0,1:T(4,128)S(1)}, s32[192,3]{0,1:T(4,128)}, u32[]{:S(2)}) copy-start(s32[192,3]{0,1:T(4,128)} %param.16) | copy-start | bytes 6916
  72.7 6.2 %copy-start.4 = (s32[192]{0:T(256)S(1)}, s32[192]{0:T(256)}, u32[]{:S(2)}) copy-start(s32[192]{0:T(256)} %param.17) | copy-start | bytes 2308
  74.6 39.3 %collective-permute-start.2 = (bf16[64,12288]{1,0:T(8,128)(2,1)}, bf16[64,12288]{1,0:T(8,128)(2,1)S(1)}, u32[]{:S(2)}, u32[]{:S(2)}) collective-permute-start(bf16[64,12288]{1,0:T(8,128)(2,1)} %get-tuple-element.5), channel_id=1, source_target_pairs={{0,4},{4,8},{8,12},{12,0},{1,5},{5,9},{9,13},{13,1},{2,6},{6,10},{... | collective-permute-start | bytes 4718600 | tf_op jit(solution)/shard_map/ppermute | solution.py:14
  76.3 70.3 %collective-permute-start.3 = (bf16[64,12288]{1,0:T(8,128)(2,1)}, bf16[64,12288]{1,0:T(8,128)(2,1)}, u32[]{:S(2)}, u32[]{:S(2)}) collective-permute-start(bf16[64,12288]{1,0:T(8,128)(2,1)} %get-tuple-element.6), channel_id=1, source_target_pairs={{4,0},{8,4},{12,8},{0,12},{5,1},{9,5},{13,9},{1,13},{6,2},{10,6},{... | collective-permute-start | bytes 4718600 | tf_op jit(solution)/shard_map/ppermute | solution.py:16
Sparse Core Ops, SparseCore 0:
  40.7 16.7 all-gather.1
where the time goes:
time: 214 us; the launch traced here: 213 us
  waiting for transfers between devices  94.5 us (44%)
  local copies, waits for them, and re-layouts  58.6 us (27%)
  matrix products  25.6 us (12%)
  between operations  13.6 us (6%)
  other arithmetic  12.1 us (6%)
  starting transfers between devices  8.99 us (4%)
    ppermute x2, waiting for transfers between devices, padded_2(): lax.ppermute(tail, axis, [(i, (i + 1) % count) for i in range(count)])  41.6 us
    ppermute x2, waiting for transfers between devices, padded_2(): lax.ppermute(head, axis, [((i + 1) % count, i) for i in range(count)])  37 us
    gather x1, local copies, waits for them, and re-layouts, dual_product(): picked = jnp.take(blocks, indices, axis=1)  23.3 us
    all_gather x1, waiting for transfers between devices, body(): refined = lax.all_gather(part_fine, 'row', axis=1, tiled=True)  15.9 us
    dot_general x1, matrix products, dual_product(): jnp.einsum('cfkb,fkbe->cfe', picked, matrices, preferred_element_type=jnp...  11.1 us
    reshape x1, other arithmetic, dual_product(): blocks = source_field.reshape(source_field.shape[0], -1, block_size)  7.75 us
    reshape x1, local copies, waits for them, and re-layouts, body(): fine_blocks = refined.reshape(columns, coarse * fine_per, block_size)  7.24 us
    dot_general x1, matrix products, body(): jnp.einsum('cib,ieb->cie', collapsed, gram_inv, preferred_element_type=jn...  6.67 us
  transfers between devices with their start and end apart: 5, of which 5 were waited for; matrix products, arithmetic and copies ran while one was open for 1% of the time, Pallas kernels for 0%

commit v1 on v0

v1 whole, which is shorter than its diff:
```python
import functools

import jax
import jax.numpy as jnp
from jax import lax
from jax.experimental import pallas as pl
from jax.experimental.pallas import tpu as pltpu
from jax.sharding import PartitionSpec as P

MESH = pl.DeviceIdType.MESH
CHUNKS = 4


def dot(a, b):
    return jnp.dot(a, b, preferred_element_type=jnp.float32)


def dot_t(a, b):
    return lax.dot_general(a, b, (((1,), (1,)), ((), ())), preferred_element_type=jnp.float32)


def spread(prolong, q):
    return jnp.concatenate([prolong[q, j] for j in range(prolong.shape[1])], axis=1)


def pick(index, live, k, spare):
    if k == 0:
        return index
    return spare + (index - spare) * lax.min(lax.max(live - k, 0), 1)


def kernel(
    parts,
    near_cols,
    dual_cols,
    dual_count,
    primal_border,
    fine_border,
    incident,
    near_hbm,
    gram_hbm,
    prolong_hbm,
    dual_hbm,
    out,
    near,
    gram,
    prolong,
    dual,
    near_field,
    rim_out,
    rim_in,
    mapped,
    fine_out,
    fine,
    load_sem,
    rim_send,
    rim_recv,
    rim_pass_send,
    rim_pass_recv,
    map_send,
    map_recv,
    fine_send,
    fine_recv,
    fine_pass_send,
    fine_pass_recv,
):
    half_rows, near_terms = near_cols.shape
    coarse, per, block, _ = prolong.shape
    terms = dual_cols.shape[1]
    columns = incident.shape[0]
    rim = primal_border.shape[2]
    rim_half = rim // 2
    fine_rim = fine_border.shape[2]
    fine_half = fine_rim // 2
    step = fine_half // CHUNKS
    own_fine = coarse * per
    row = lax.axis_index("row")
    surf = lax.axis_index("surf")
    sibling = {"row": 1 - row}
    neighbours = (
        {"surf": lax.rem(surf + parts - 1, parts)},
        {"surf": lax.rem(surf + 1, parts)},
    )

    moves = [(near_hbm, near), (gram_hbm, gram), (dual_hbm, dual)] + [
        (prolong_hbm.at[:, :, pl.ds(j * block, block)], prolong.at[:, j]) for j in range(per)
    ]
    loads = [
        pltpu.make_async_copy(src, dst, load_sem.at[i]) for i, (src, dst) in enumerate(moves)
    ]
    for load in loads:
        load.start()

    barrier = pltpu.get_barrier_semaphore()
    for device in neighbours + (sibling,):
        pl.semaphore_signal(barrier, inc=1, device_id=device, device_id_type=MESH)

    def lay(j, carry):
        near_field[j] = incident[:, pl.ds(pl.multiple_of(j * block, block), block)]
        return carry

    lax.fori_loop(0, coarse, lay, 0, unroll=4)
    for way in range(2):

        def pack(j, carry, way=way):
            at = primal_border[0, way, row * rim_half + j]
            rim_out[way, j] = near_field[at]
            return carry

        lax.fori_loop(0, rim_half, pack, 0, unroll=True)

    pl.semaphore_wait(barrier, 3)

    rim_copies = [
        pltpu.make_async_remote_copy(
            src_ref=rim_out.at[way],
            dst_ref=rim_in.at[1 - way, row],
            send_sem=rim_send.at[way],
            recv_sem=rim_recv.at[1 - way],
            device_id=neighbours[way],
            device_id_type=MESH,
        )
        for way in range(2)
    ]
    for copy in rim_copies:
        copy.start()

    fine[own_fine + 2 * fine_rim] = jnp.zeros((columns, block), jnp.bfloat16)

    rim_passes = []
    for way in range(2):
        rim_copies[way].wait_recv()
        copy = pltpu.make_async_remote_copy(
            src_ref=rim_in.at[1 - way, row],
            dst_ref=rim_in.at[1 - way, row],
            send_sem=rim_pass_send.at[way],
            recv_sem=rim_pass_recv.at[way],
            device_id=sibling,
            device_id_type=MESH,
        )
        copy.start()
        rim_passes.append(copy)
    for copy in rim_passes:
        copy.wait_recv()
    for side in range(2):
        for half in range(2):
            for j in range(rim_half):
                near_field[coarse + side * rim + half * rim_half + j] = rim_in[side, half, j]

    loads[0].wait()
    loads[1].wait()
    map_copies = []
    map_step = half_rows // CHUNKS
    for chunk in range(CHUNKS):

        def primal(i, carry):
            picked = jnp.concatenate([near_field[near_cols[i, k]] for k in range(near_terms)], axis=1)
            applied = dot(picked, near[i].reshape(near_terms * block, block)).astype(jnp.bfloat16)
            mapped[row * half_rows + i] = dot(applied, gram[i]).astype(jnp.bfloat16)
            return carry

        lax.fori_loop(chunk * map_step, (chunk + 1) * map_step, primal, 0, unroll=4)
        span = pl.ds(row * half_rows + chunk * map_step, map_step)
        copy = pltpu.make_async_remote_copy(
            src_ref=mapped.at[span],
            dst_ref=mapped.at[span],
            send_sem=map_send.at[chunk],
            recv_sem=map_recv.at[chunk],
            device_id=sibling,
            device_id_type=MESH,
        )
        copy.start()
        map_copies.append(copy)

    for load in loads[3:]:
        load.wait()
    for copy in map_copies:
        copy.wait()

    fine_copies = []
    for chunk in range(CHUNKS):
        for way in range(2):

            def border(j, carry, way=way):
                at = fine_border[0, way, row * fine_half + j]
                source = lax.div(at, per)
                fine_out[way, j] = dot(
                    mapped[source], prolong[source, at - source * per]
                ).astype(jnp.bfloat16)
                return carry

            lax.fori_loop(chunk * step, (chunk + 1) * step, border, 0, unroll=4)
            copy = pltpu.make_async_remote_copy(
                src_ref=fine_out.at[way, pl.ds(chunk * step, step)],
                dst_ref=fine.at[
                    pl.ds(own_fine + (1 - way) * fine_rim + row * fine_half + chunk * step, step)
                ],
                send_sem=fine_send.at[way, chunk],
                recv_sem=fine_recv.at[1 - way, chunk],
                device_id=neighbours[way],
                device_id_type=MESH,
            )
            copy.start()
            fine_copies.append((way, chunk, copy))

    def refine(q, carry):
        result = dot(mapped[q], spread(prolong, q)).astype(jnp.bfloat16)
        for j in range(per):
            fine[q * per + j] = result[:, j * block : (j + 1) * block]
        return carry

    lax.fori_loop(0, coarse, refine, 0, unroll=2)
    loads[2].wait()

    fine_passes = []
    for way, chunk, arrived in fine_copies:
        arrived.wait_recv()
        span = pl.ds(own_fine + (1 - way) * fine_rim + row * fine_half + chunk * step, step)
        copy = pltpu.make_async_remote_copy(
            src_ref=fine.at[span],
            dst_ref=fine.at[span],
            send_sem=fine_pass_send.at[way, chunk],
            recv_sem=fine_pass_recv.at[way, chunk],
            device_id=sibling,
            device_id_type=MESH,
        )
        copy.start()
        fine_passes.append(copy)
    for copy in fine_passes:
        copy.wait()

    def collapse(i, carry):
        pieces = []
        for j in range(per):
            f = i * per + j
            live = dual_count[f]
            picked = jnp.concatenate(
                [
                    fine[pick(dual_cols[f, k], live, k, own_fine + 2 * fine_rim)]
                    for k in range(terms)
                ],
                axis=1,
            )
            pieces.append(dot(picked, dual[f].reshape(terms * block, block)).astype(jnp.bfloat16))
        response = jnp.concatenate(pieces, axis=1)
        collapsed = dot_t(response, spread(prolong, row * half_rows + i)).astype(jnp.bfloat16)
        out[:, pl.ds(pl.multiple_of(i * block, block), block)] = dot_t(collapsed, gram[i])
        return carry

    lax.fori_loop(0, half_rows, collapse, 0, unroll=2)

    for copy in rim_copies + rim_passes:
        copy.wait_send()
    for _, _, copy in fine_copies:
        copy.wait_send()


def body(
    parts,
    incident,
    near_blocks,
    near_cols,
    gram_inv,
    prolong,
    dual_blocks,
    dual_cols,
    dual_count,
    primal_border,
    fine_border,
):
    columns = incident.shape[0]
    coarse, block, wide = prolong.shape
    per = wide // block
    half_rows = near_blocks.shape[0]
    rim = primal_border.shape[2]
    fine_rim = fine_border.shape[2]
    cell = (columns, block)
    low = jnp.bfloat16
    smem = pl.BlockSpec(memory_space=pltpu.SMEM)
    vmem = pl.BlockSpec(memory_space=pltpu.VMEM)
    hbm = pl.BlockSpec(memory_space=pl.ANY)
    sems = pltpu.SemaphoreType.DMA
    return pl.pallas_call(
        functools.partial(kernel, parts),
        out_shape=jax.ShapeDtypeStruct((columns, half_rows * block), jnp.float32),
        in_specs=[smem] * 5 + [vmem] + [hbm] * 4,
        out_specs=vmem,
        scratch_shapes=[
            pltpu.VMEM(near_blocks.shape, low),
            pltpu.VMEM(gram_inv.shape, low),
            pltpu.VMEM((coarse, per, block, block), low),
            pltpu.VMEM(dual_blocks.shape, low),
            pltpu.VMEM((coarse + 2 * rim,) + cell, low),
            pltpu.VMEM((2, rim // 2) + cell, low),
            pltpu.VMEM((2, 2, rim // 2) + cell, low),
            pltpu.VMEM((coarse,) + cell, low),
            pltpu.VMEM((2, fine_rim // 2) + cell, low),
            pltpu.VMEM((coarse * per + 2 * fine_rim + 1,) + cell, low),
            sems((3 + per,)),
            sems((2,)),
            sems((2,)),
            sems((2,)),
            sems((2,)),
            sems((CHUNKS,)),
            sems((CHUNKS,)),
            sems((2, CHUNKS)),
            sems((2, CHUNKS)),
            sems((2, CHUNKS)),
            sems((2, CHUNKS)),
        ],
        compiler_params=pltpu.CompilerParams(
            collective_id=0, has_side_effects=True, vmem_limit_bytes=60 * 2**20
        ),
    )(
        near_cols,
        dual_cols,
        dual_count,
        primal_border,
        fine_border,
        incident,
        near_blocks,
        gram_inv,
        prolong,
        dual_blocks,
    )


def solution(mesh):
    return jax.shard_map(
        functools.partial(body, mesh.shape["surf"]),
        mesh=mesh,
        in_specs=(
            P(("grp", "ang"), "surf"),
            P(("grp", "surf", "row"), None, None, None),
            P(("grp", "surf", "row"), None),
            P(("grp", "surf", "row"), None, None),
            P(("grp", "surf"), None, None),
            P(("grp", "surf", "row"), None, None, None),
            P(("grp", "surf", "row"), None),
            P(("grp", "surf", "row")),
            P(("grp", "surf"), None, None),
            P(("grp", "surf"), None, None),
        ),
        out_specs=P(("grp", "ang"), ("surf", "row")),
        check_vma=False,
    )
```

time: 214 us -> 81.4 us (0.38)
  waiting for transfers between devices: 94.5 us -> 0 us
  Pallas kernels: 0 us -> 76 us
  local copies, waits for them, and re-layouts: 58.6 us -> 5.08 us
  matrix products: 25.6 us -> 0 us
  between operations: 13.6 us -> 0.01 us
  other arithmetic: 12.1 us -> 0 us
  starting transfers between devices: 8.99 us -> 0 us
    ppermute x4 -> x0, waiting for transfers between devices: 78.6 us -> none  [the longest x2 41.6 us: padded_2(): lax.ppermute(tail, axis, [(i, (i + 1) % count) for i in range(count)])]
    pallas_call x0 -> x1, Pallas kernels: none -> 76 us  [body(): pl.pallas_call(functools.partial(kernel, parts), out_shape=jax.ShapeDtype...]
    gather x4 -> x0, local copies, waits for them, and re-layouts: 31.7 us -> none  [the longest x1 23.3 us: dual_product(): picked = jnp.take(blocks, indices, axis=1)]
    dot_general x4 -> x0, matrix products: 25.6 us -> none  [the longest x1 11.1 us: dual_product(): jnp.einsum('cfkb,fkbe->cfe', picked, matrices, preferred_element_type=jnp...]
    reshape x5 -> x0, local copies, waits for them, and re-layouts: 18 us -> none  [the longest x1 7.24 us: body(): fine_blocks = refined.reshape(columns, coarse * fine_per, block_size)]
    all_gather x1 -> x0, waiting for transfers between devices: 15.9 us -> none  [body(): refined = lax.all_gather(part_fine, 'row', axis=1, tiled=True)]
    reshape x2 -> x0, other arithmetic: 9.42 us -> none  [the longest x1 7.75 us: dual_product(): blocks = source_field.reshape(source_field.shape[0], -1, block_size)]
    ppermute x4 -> x0, starting transfers between devices: 8.99 us -> none  [the longest x2 4.82 us: padded_2(): lax.ppermute(tail, axis, [(i, (i + 1) % count) for i in range(count)])]
  transfers between devices with their start and end apart: 5 -> 0, of which waited for: 5 -> 0; matrix products, arithmetic and copies ran while one was open for 1% -> 0% of each run, Pallas kernels for 0% -> 0%
where the time goes in v1:
time: 81.4 us; the launch traced here: 81.1 us
  Pallas kernels  76 us (93%)
  local copies, waits for them, and re-layouts  5.08 us (6%)
    pallas_call x1, Pallas kernels, body(): pl.pallas_call(functools.partial(kernel, parts), out_shape=jax.ShapeDtype...  76 us
    unnamed x3, local copies, waits for them, and re-layouts  5.08 us

profile of v1, /device:TPU:0, one launch (start us, length us, event | category | flops | bytes accessed | tf_op | source)
XLA Modules:
  0.0 81.1 jit_solution(14586206585716941636)
XLA Ops:
  0.0 1.4 %copy.11.near_cols = s32[32,4]{1,0:T(8,128)} copy(s32[32,4]{0,1:T(4,128)} %param.12) | data formatting | bytes 1024 | tf_op args[2]
  1.4 1.4 %copy.12.dual_cols = s32[192,3]{1,0:T(8,128)} copy(s32[192,3]{0,1:T(4,128)} %param.16) | data formatting | bytes 4608 | tf_op args[6]
  2.8 76.0 %shard_map.100 = f32[64,4096]{1,0:T(8,128)} custom-call(s32[32,4]{1,0:T(8,128)} %copy.11.near_cols, s32[192,3]{1,0:T(8,128)} %copy.12.dual_cols, s32[192]{0:T(256)} %dual_count.1, s32[1,2,16]{2,1,0:T(2,128)} %primal_border.1, s32[1,2,96]{2,1,0:T(2,128)} %fine_border.1, bf16[64,8192]{1,0:T(8,128)(2,1)} %incident.1, bf16[32,4,128,128]{3,2,1,0:T(8,128)(2,1)} %near_hbm.1, ...), custom_call_target="tpu_custom_call" | custom-call | tf_op jit(solution)/shard_map/pallas_call | solution.py:283
  78.9 2.3 %copy.14 = f32[64,4096]{1,0:T(8,128)} copy(f32[64,4096]{1,0:T(8,128)} %shard_map.100) | data formatting | bytes 2097152

commit v2 on v1

--- a/solution.py
+++ b/solution.py
@@ -64,9 +64,9 @@
     fine_pass_send,
     fine_pass_recv,
 ):
-    half_rows, near_terms = near_cols.shape
+    near_terms, half_rows = near_cols.shape
     coarse, per, block, _ = prolong.shape
-    terms = dual_cols.shape[1]
+    terms = dual_cols.shape[0]
     columns = incident.shape[0]
     rim = primal_border.shape[2]
     rim_half = rim // 2
@@ -82,9 +82,9 @@
         {"surf": lax.rem(surf + 1, parts)},
     )
 
-    moves = [(near_hbm, near), (gram_hbm, gram), (dual_hbm, dual)] + [
-        (prolong_hbm.at[:, :, pl.ds(j * block, block)], prolong.at[:, j]) for j in range(per)
-    ]
+    moves = [(gram_hbm, gram), (near_hbm, near)]
+    moves += [(prolong_hbm.at[:, :, pl.ds(j * block, block)], prolong.at[:, j]) for j in range(per)]
+    moves += [(dual_hbm, dual)]
     loads = [
         pltpu.make_async_copy(src, dst, load_sem.at[i]) for i, (src, dst) in enumerate(moves)
     ]
@@ -126,6 +126,16 @@
         copy.start()
 
     fine[own_fine + 2 * fine_rim] = jnp.zeros((columns, block), jnp.bfloat16)
+
+    loads[0].wait()
+    loads[1].wait()
+
+    def combine_near(i, carry):
+        joined = dot(near[i].reshape(near_terms * block, block), gram[i]).astype(jnp.bfloat16)
+        near[i] = joined.reshape(near_terms, block, block)
+        return carry
+
+    lax.fori_loop(0, half_rows, combine_near, 0, unroll=2)
 
     rim_passes = []
     for way in range(2):
@@ -147,16 +157,15 @@
             for j in range(rim_half):
                 near_field[coarse + side * rim + half * rim_half + j] = rim_in[side, half, j]
 
-    loads[0].wait()
-    loads[1].wait()
     map_copies = []
     map_step = half_rows // CHUNKS
     for chunk in range(CHUNKS):
 
         def primal(i, carry):
-            picked = jnp.concatenate([near_field[near_cols[i, k]] for k in range(near_terms)], axis=1)
-            applied = dot(picked, near[i].reshape(near_terms * block, block)).astype(jnp.bfloat16)
-            mapped[row * half_rows + i] = dot(applied, gram[i]).astype(jnp.bfloat16)
+            picked = jnp.concatenate([near_field[near_cols[k, i]] for k in range(near_terms)], axis=1)
+            mapped[row * half_rows + i] = dot(
+                picked, near[i].reshape(near_terms * block, block)
+            ).astype(jnp.bfloat16)
             return carry
 
         lax.fori_loop(chunk * map_step, (chunk + 1) * map_step, primal, 0, unroll=4)
@@ -172,7 +181,7 @@
         copy.start()
         map_copies.append(copy)
 
-    for load in loads[3:]:
+    for load in loads[2:-1]:
         load.wait()
     for copy in map_copies:
         copy.wait()
@@ -210,7 +219,19 @@
         return carry
 
     lax.fori_loop(0, coarse, refine, 0, unroll=2)
-    loads[2].wait()
+    loads[-1].wait()
+
+    def combine_dual(i, carry):
+        back = dot(gram[i], spread(prolong, row * half_rows + i)).astype(jnp.bfloat16)
+        for j in range(per):
+            f = i * per + j
+            joined = dot_t(
+                dual[f].reshape(terms * block, block), back[:, j * block : (j + 1) * block]
+            ).astype(jnp.bfloat16)
+            dual[f] = joined.reshape(terms, block, block)
+        return carry
+
+    lax.fori_loop(0, half_rows, combine_dual, 0)
 
     fine_passes = []
     for way, chunk, arrived in fine_copies:
@@ -229,22 +250,18 @@
     for copy in fine_passes:
         copy.wait()
 
+    spare = own_fine + 2 * fine_rim
+
     def collapse(i, carry):
-        pieces = []
+        picked = []
         for j in range(per):
             f = i * per + j
             live = dual_count[f]
-            picked = jnp.concatenate(
-                [
-                    fine[pick(dual_cols[f, k], live, k, own_fine + 2 * fine_rim)]
-                    for k in range(terms)
-                ],
-                axis=1,
-            )
-            pieces.append(dot(picked, dual[f].reshape(terms * block, block)).astype(jnp.bfloat16))
-        response = jnp.concatenate(pieces, axis=1)
-        collapsed = dot_t(response, spread(prolong, row * half_rows + i)).astype(jnp.bfloat16)
-        out[:, pl.ds(pl.multiple_of(i * block, block), block)] = dot_t(collapsed, gram[i])
+            picked += [fine[pick(dual_cols[k, f], live, k, spare)] for k in range(terms)]
+        joined = dual[pl.ds(i * per, per)].reshape(per * terms * block, block)
+        out[:, pl.ds(pl.multiple_of(i * block, block), block)] = dot(
+            jnp.concatenate(picked, axis=1), joined
+        )
         return carry
 
     lax.fori_loop(0, half_rows, collapse, 0, unroll=2)
@@ -312,8 +329,8 @@
             collective_id=0, has_side_effects=True, vmem_limit_bytes=60 * 2**20
         ),
     )(
-        near_cols,
-        dual_cols,
+        near_cols.T,
+        dual_cols.T,
         dual_count,
         primal_border,
         fine_border,

time: 81.4 us -> 64.7 us (0.79)
  Pallas kernels: 76 us -> 62.3 us
  local copies, waits for them, and re-layouts: 5.08 us -> 2.27 us
    pallas_call x1, Pallas kernels: 76 us -> 62.3 us  [body(): pl.pallas_call(functools.partial(kernel, parts), out_shape=jax.ShapeDtype...]
    unnamed x3 -> x1, local copies, waits for them, and re-layouts: 5.08 us -> 2.27 us
where the time goes in v2:
time: 64.7 us; the launch traced here: 64.6 us
  Pallas kernels  62.3 us (96%)
  local copies, waits for them, and re-layouts  2.27 us (4%)
    pallas_call x1, Pallas kernels, body(): pl.pallas_call(functools.partial(kernel, parts), out_shape=jax.ShapeDtype...  62.3 us
    unnamed x1, local copies, waits for them, and re-layouts  2.27 us

profile of v2, /device:TPU:0, one launch (start us, length us, event | category | flops | bytes accessed | tf_op | source)
XLA Modules:
  0.0 64.6 jit_solution(14111148628021629321)
XLA Ops:
  0.0 62.3 %shard_map.100 = f32[64,4096]{1,0:T(8,128)} custom-call(s32[4,32]{1,0:T(4,128)} %bitcast.3, s32[3,192]{1,0:T(4,128)} %bitcast.2, s32[192]{0:T(256)} %dual_count.1, s32[1,2,16]{2,1,0:T(2,128)} %primal_border.1, s32[1,2,96]{2,1,0:T(2,128)} %fine_border.1, bf16[64,8192]{1,0:T(8,128)(2,1)} %incident.1, bf16[32,4,128,128]{3,2,1,0:T(8,128)(2,1)} %near_hbm.1, ...), custom_call_target="tpu_custom_call" | custom-call | tf_op jit(solution)/shard_map/pallas_call | solution.py:300
  62.3 2.3 %copy.12 = f32[64,4096]{1,0:T(8,128)} copy(f32[64,4096]{1,0:T(8,128)} %shard_map.100) | data formatting | bytes 2097152

commit v3 on v2

--- a/solution.py
+++ b/solution.py
@@ -8,7 +8,9 @@
 from jax.sharding import PartitionSpec as P
 
 MESH = pl.DeviceIdType.MESH
-CHUNKS = 4
+CHUNKS = 6
+MAP_CHUNKS = 4
+OUT_CHUNKS = 4
 
 
 def dot(a, b):
@@ -31,16 +33,22 @@
 
 def kernel(
     parts,
-    near_cols,
-    dual_cols,
-    dual_count,
+    near_cols_hbm,
+    dual_cols_hbm,
+    dual_count_hbm,
     primal_border,
-    fine_border,
-    incident,
+    fine_border_hbm,
+    incident_hbm,
     near_hbm,
     gram_hbm,
     prolong_hbm,
     dual_hbm,
+    out_hbm,
+    near_cols,
+    dual_cols,
+    dual_count,
+    fine_border,
+    incident,
     out,
     near,
     gram,
@@ -53,6 +61,8 @@
     fine_out,
     fine,
     load_sem,
+    table_sem,
+    out_sem,
     rim_send,
     rim_recv,
     rim_pass_send,
@@ -82,6 +92,26 @@
         {"surf": lax.rem(surf + 1, parts)},
     )
 
+    barrier = pltpu.get_barrier_semaphore()
+    for device in neighbours + (sibling,):
+        pl.semaphore_signal(barrier, inc=1, device_id=device, device_id_type=MESH)
+
+    opening = pltpu.make_async_copy(incident_hbm, incident, table_sem.at[0])
+    opening.start()
+    tables = [
+        pltpu.make_async_copy(src, dst, table_sem.at[1 + i])
+        for i, (src, dst) in enumerate(
+            (
+                (near_cols_hbm, near_cols),
+                (fine_border_hbm, fine_border),
+                (dual_cols_hbm, dual_cols),
+                (dual_count_hbm, dual_count),
+            )
+        )
+    ]
+    for table in tables:
+        table.start()
+
     moves = [(gram_hbm, gram), (near_hbm, near)]
     moves += [(prolong_hbm.at[:, :, pl.ds(j * block, block)], prolong.at[:, j]) for j in range(per)]
     moves += [(dual_hbm, dual)]
@@ -91,9 +121,7 @@
     for load in loads:
         load.start()
 
-    barrier = pltpu.get_barrier_semaphore()
-    for device in neighbours + (sibling,):
-        pl.semaphore_signal(barrier, inc=1, device_id=device, device_id_type=MESH)
+    opening.wait()
 
     def lay(j, carry):
         near_field[j] = incident[:, pl.ds(pl.multiple_of(j * block, block), block)]
@@ -157,9 +185,11 @@
             for j in range(rim_half):
                 near_field[coarse + side * rim + half * rim_half + j] = rim_in[side, half, j]
 
+    for table in tables:
+        table.wait()
     map_copies = []
-    map_step = half_rows // CHUNKS
-    for chunk in range(CHUNKS):
+    map_step = half_rows // MAP_CHUNKS
+    for chunk in range(MAP_CHUNKS):
 
         def primal(i, carry):
             picked = jnp.concatenate([near_field[near_cols[k, i]] for k in range(near_terms)], axis=1)
@@ -264,12 +294,21 @@
         )
         return carry
 
-    lax.fori_loop(0, half_rows, collapse, 0, unroll=2)
+    out_step = half_rows // OUT_CHUNKS
+    results = []
+    for chunk in range(OUT_CHUNKS):
+        lax.fori_loop(chunk * out_step, (chunk + 1) * out_step, collapse, 0, unroll=4)
+        span = pl.ds(chunk * out_step * block, out_step * block)
+        result = pltpu.make_async_copy(out.at[:, span], out_hbm.at[:, span], out_sem.at[chunk])
+        result.start()
+        results.append(result)
 
     for copy in rim_copies + rim_passes:
         copy.wait_send()
     for _, _, copy in fine_copies:
         copy.wait_send()
+    for result in results:
+        result.wait()
 
 
 def body(
@@ -294,15 +333,20 @@
     cell = (columns, block)
     low = jnp.bfloat16
     smem = pl.BlockSpec(memory_space=pltpu.SMEM)
-    vmem = pl.BlockSpec(memory_space=pltpu.VMEM)
     hbm = pl.BlockSpec(memory_space=pl.ANY)
     sems = pltpu.SemaphoreType.DMA
     return pl.pallas_call(
         functools.partial(kernel, parts),
         out_shape=jax.ShapeDtypeStruct((columns, half_rows * block), jnp.float32),
-        in_specs=[smem] * 5 + [vmem] + [hbm] * 4,
-        out_specs=vmem,
+        in_specs=[hbm] * 3 + [smem] + [hbm] * 6,
+        out_specs=hbm,
         scratch_shapes=[
+            pltpu.SMEM(near_cols.shape[::-1], jnp.int32),
+            pltpu.SMEM(dual_cols.shape[::-1], jnp.int32),
+            pltpu.SMEM(dual_count.shape, jnp.int32),
+            pltpu.SMEM(fine_border.shape, jnp.int32),
+            pltpu.VMEM(incident.shape, low),
+            pltpu.VMEM((columns, half_rows * block), jnp.float32),
             pltpu.VMEM(near_blocks.shape, low),
             pltpu.VMEM(gram_inv.shape, low),
             pltpu.VMEM((coarse, per, block, block), low),
@@ -314,12 +358,14 @@
             pltpu.VMEM((2, fine_rim // 2) + cell, low),
             pltpu.VMEM((coarse * per + 2 * fine_rim + 1,) + cell, low),
             sems((3 + per,)),
+            sems((5,)),
+            sems((OUT_CHUNKS,)),
             sems((2,)),
             sems((2,)),
             sems((2,)),
             sems((2,)),
-            sems((CHUNKS,)),
-            sems((CHUNKS,)),
+            sems((MAP_CHUNKS,)),
+            sems((MAP_CHUNKS,)),
             sems((2, CHUNKS)),
             sems((2, CHUNKS)),
             sems((2, CHUNKS)),

time: 64.7 us -> 62.5 us (0.966)
  Pallas kernels: 62.3 us -> 60 us
    pallas_call x1, Pallas kernels: 62.3 us -> 60 us  [body(): pl.pallas_call(functools.partial(kernel, parts), out_shape=jax.ShapeDtype...]
where the time goes in v3:
time: 62.5 us; the launch traced here: 62.3 us
  Pallas kernels  60 us (96%)
  local copies, waits for them, and re-layouts  2.27 us (4%)
    pallas_call x1, Pallas kernels, body(): pl.pallas_call(functools.partial(kernel, parts), out_shape=jax.ShapeDtype...  60 us
    unnamed x1, local copies, waits for them, and re-layouts  2.27 us

profile of v3, /device:TPU:0, one launch (start us, length us, event | category | flops | bytes accessed | tf_op | source)
XLA Modules:
  0.0 62.3 jit_solution(3193224303969503018)
XLA Ops:
  0.0 60.0 %shard_map.100 = f32[64,4096]{1,0:T(8,128)} custom-call(s32[4,32]{1,0:T(4,128)} %bitcast.3, s32[3,192]{1,0:T(4,128)} %bitcast.2, s32[192]{0:T(256)} %dual_count_hbm.1, s32[1,2,16]{2,1,0:T(2,128)} %primal_border.1, s32[1,2,96]{2,1,0:T(2,128)} %fine_border_hbm.1, bf16[64,8192]{1,0:T(8,128)(2,1)} %incident_hbm.1, bf16[32,4,128,128]{3,2,1,0:T(8,128)(2,1)} %near_hbm.1, ...), custom_call_target="tpu_custom_call" | custom-call | tf_op jit(solution)/shard_map/pallas_call | solution.py:338
  60.0 2.3 %copy.12 = f32[64,4096]{1,0:T(8,128)} copy(f32[64,4096]{1,0:T(8,128)} %shard_map.100) | data formatting | bytes 2097152
